TPU v7x, 128 devices: a whole 4x4x4 slice. The times are simulated.
128 devices in a mesh: blk: 16 (over x, z_lo, core), grp: 8 (over y, z_hi).
Axes of the slice: x: 4, y: 4, z: 4 (z_hi: 2, z_lo: 2; z = z_hi * 2 + z_lo), core: 2. Of those that a mesh axis runs over, the one named last changes fastest.
Arguments:
- right_vector: bfloat16 [768, 1, 32, 768], P(None, None, 'blk'), may hold values from -10 to 10
- left_vector: bfloat16 [768, 1, 32, 768], P('blk', None, 'grp'), may hold values from -14 to 14
- cycle_weights: bfloat16 [32, 32, 768, 768], P('blk', 'grp'), may hold values from -1 to 4
- screen: int32 [1, 32], replicated, may hold values 0 or 1
Outputs:
- sigma_right: float32 [768, 1, 32, 768], P('blk', None, 'grp')
- sigma_left: float32 [768, 1, 32, 768], P('grp', None, 'blk')
- rayleigh: float32 [1], replicated
All inputs are finite; a program needn't handle non-finite values.
Results may differ from a plain program's by a relative error of at most 0.0003.
Values may be sent and summed in bfloat16 or wider, within the bound.
A program may use at most 128 MiB of HBM per device.

v0:
```python
import jax
import jax.numpy as jnp
from jax import lax
from jax.sharding import PartitionSpec as P


def body(right_vector, left_vector, cycle_weights, screen):
    position = lax.axis_index("blk")
    group_index = lax.axis_index("grp")
    occ_here = cycle_weights.shape[0]
    group_width = cycle_weights.shape[1]
    vir_count = right_vector.shape[0]
    trial_rows = right_vector.shape[1]
    screen_cols = lax.dynamic_slice_in_dim(screen, position * occ_here, occ_here, 1).astype(
        jnp.float32
    )
    screened_right = right_vector * screen_cols[None, :, :, None].astype(jnp.bfloat16)
    occ_ids = position * occ_here + jnp.arange(occ_here, dtype=jnp.int32)
    pair_ids = group_index * group_width + jnp.arange(group_width, dtype=jnp.int32)
    selector = (pair_ids[:, None] == occ_ids[None, :]).astype(jnp.float32)
    piece_rows = lax.all_gather(left_vector, "blk", axis=0, tiled=True)
    row_count = piece_rows.shape[0]
    flat_rows = piece_rows.reshape(row_count * trial_rows, group_width, vir_count)
    product = jnp.einsum(
        "kjb,mjeb->kme", flat_rows, cycle_weights, preferred_element_type=jnp.float32
    )
    product = product.reshape(row_count, trial_rows, occ_here, vir_count)
    paired = jnp.einsum(
        "aijb,aimb->jm", piece_rows, right_vector, preferred_element_type=jnp.float32
    )
    correlation = jnp.sum(paired * selector)
    sigma_right = lax.psum_scatter(
        jnp.einsum(
            "aime,mjeb->aijb", screened_right, cycle_weights, preferred_element_type=jnp.float32
        ),
        "blk",
        scatter_dimension=0,
        tiled=True,
    )
    sigma_left = (
        lax.psum_scatter(product, "grp", scatter_dimension=0, tiled=True)
        * screen_cols[None, :, :, None]
    )
    numerator_part = jnp.sum(sigma_right * left_vector.astype(jnp.float32))
    numerator, denominator = lax.psum((numerator_part, correlation), ("blk", "grp"))
    rayleigh = (numerator / denominator).reshape(1)
    return (sigma_right, sigma_left, rayleigh)


def solution(mesh):
    in_specs = (
        P(None, None, "blk", None),
        P("blk", None, "grp", None),
        P("blk", "grp", None, None),
        P(),
    )
    out_specs = (P("blk", None, "grp", None), P("grp", None, "blk", None), P())
    return jax.shard_map(body, mesh=mesh, in_specs=in_specs, out_specs=out_specs, check_vma=False)
```

profile of v0, /device:TPU:0, one launch (start us, length us, event | category | flops | bytes accessed | tf_op | source)
XLA Modules:
  0.0 341.3 jit_solution(10437045412615822093)
XLA Ops:
  7.2 0.0 all-gather.2.cloned.1.call-start
  7.2 1.7 copy.9
  8.9 0.0 all-gather.2.cloned.1.call-update
  8.9 0.0 reduce-scatter.5.cloned.1.call-start
  9.0 42.0 %all-gather.2.cloned.1.call-done = bf16[768,1,4,768]{3,0,2,1:T(8,128)(2,1)} async-done(((bf16[48,1,4,768]{3,0,2,1:T(8,128)(2,1)}), bf16[768,1,4,768]{3,0,2,1:T(8,128)(2,1)}) %all-gather.2.cloned.1.call-update) | async-done | bytes 4718608 | tf_op jit(solution)/shard_map/all_gather | solution.py:21
  51.0 12.9 %fusion.7 = f32[768,1,2,768]{3,0,2,1:T(8,128)} fusion(bf16[2,4,768,768]{3,2,1,0:T(8,128)(2,1)} %param.6, bf16[768,1,4,768]{3,0,2,1:T(8,128)(2,1)} %all-gather.2.cloned.1.call-done), kind=kOutput, calls=%fused_computation.9 | convolution fusion | flops 7247757312 | bytes 18874368 | tf_op jit(solution)/shard_map/kjb,mjeb->kme/dot_general | solution.py:24
  63.9 0.0 reduce-scatter.5.cloned.1.call-update
  64.0 0.2 reduce-scatter.3.cloned.1.call-start
  64.2 0.4 copy-done.2
  64.6 0.1 fusion.25
  64.7 1.0 copy-done
  65.6 2.1 multiply_bitcast_fusion
  67.7 12.2 %convolution_bitcast_fusion = f32[768,1,4,768]{3,0,2,1:T(8,128)} fusion(bf16[2,4,768,768]{3,2,1,0:T(8,128)(2,1)} %param.6, bf16[768,2,768]{2,1,0:T(2,128)(2,1)S(1)} %multiply_bitcast_fusion), kind=kOutput, calls=%fused_computation.4 | convolution fusion | flops 7247757312 | bytes 21233664 | tf_op jit(solution)/shard_map/aime,mjeb->aijb/dot_general | solution.py:33
  79.9 0.0 reduce-scatter.3.cloned.1.call-update
  80.0 0.0 copy-start.1
  80.0 10.9 %fusion.20 = f32[]{:T(128)} fusion(bf16[768,1,2,768]{3,2,1,0:T(2,128)(2,1)S(1)} %copy-done, bf16[768,4,768]{2,0,1:T(8,128)(2,1)} %bitcast.44, s32[4]{0:T(128)S(1)} %iota_add_fusion.1, s32[2]{0:T(128)S(1)} %iota_add_fusion), kind=kOutput, calls=%fused_computation.13 | convolution fusion | flops 9437207 | bytes 7077916 | tf_op jit(solution)/shard_map/aijb,aimb->jm/dot_general | solution.py:28
  90.9 62.0 %reduce-scatter.5.cloned.1.call-done = f32[96,1,2,768]{3,0,2,1:T(8,128)} async-done(((f32[768,1,2,768]{3,0,2,1:T(8,128)}), f32[96,1,2,768]{3,0,2,1:T(8,128)}) %reduce-scatter.5.cloned.1.call-update) | async-done | bytes 589840 | tf_op jit(solution)/shard_map/reduce_scatter | solution.py:41
  152.9 1.2 broadcast_multiply_fusion
  154.1 104.3 %reduce-scatter.3.cloned.1.call-done = f32[48,1,4,768]{3,0,2,1:T(8,128)} async-done(((f32[768,1,4,768]{3,0,2,1:T(8,128)}), f32[48,1,4,768]{3,0,2,1:T(8,128)}) %reduce-scatter.3.cloned.1.call-update) | async-done | bytes 589840 | tf_op jit(solution)/shard_map/reduce_scatter | solution.py:32
  258.4 0.0 copy-done.1
  258.4 1.8 multiply_reduce_fusion
  260.2 1.3 copy.13
  261.5 68.5 %all-reduce = (f32[]{:T(128)}, f32[]{:T(128)}) all-reduce(f32[]{:T(128)} %multiply_reduce_fusion, f32[]{:T(128)} %fusion.20), channel_id=1, replica_groups=mesh['blk'=16,'grp'=8] {'blk','grp'}, use_global_device_ids=true, to_apply=%region_3.0 | all-reduce | flops 2 | bytes 16 | tf_op jit(solution)/shard_map/psum | solution.py:45
  331.3 2.3 copy.12
  (4 shorter events, 0.0 us)
Async XLA Ops:
  7.2 43.9 %all-gather.2.cloned.1.call-start = ((), (), s32[]{:S(2)}) async-start(), calls=%async_computation.3 | async-start | bytes 5013504 | tf_op jit(solution)/shard_map/all_gather | solution.py:21
  8.9 144.0 %reduce-scatter.5.cloned.1.call-start = ((), (), s32[]{:S(2)}) async-start(), calls=%async_computation.4 | async-start | bytes 5308416 | tf_op jit(solution)/shard_map/reduce_scatter | solution.py:41
  63.9 0.7 copy-start.2
  63.9 1.7 copy-start
  64.0 194.4 %reduce-scatter.3.cloned.1.call-start = ((), (), s32[]{:S(2)}) async-start(), calls=%async_computation.2 | async-start | bytes 10027008 | tf_op jit(solution)/shard_map/reduce_scatter | solution.py:32
  80.0 178.4 %copy-start.1 = (bf16[48,1,4,768]{3,2,1,0:T(4,128)(2,1)S(1)}, bf16[48,1,4,768]{3,2,1,0:T(4,128)(2,1)}, u32[]{:S(2)}) copy-start(bf16[48,1,4,768]{3,2,1,0:T(4,128)(2,1)} %param.5) | copy-start | bytes 884740
Sparse Core Ops, SparseCore 0:
  10.2 40.7 all-gather.1
  64.1 88.7 reduce-scatter.4
  155.5 102.8 reduce-scatter.2
where the time goes:
time: 342 us; the launch traced here: 341 us
  waiting for transfers between devices  208 us (61%)
  blocking collectives  68.5 us (20%)
  matrix products  36 us (11%)
  between operations  16.3 us (5%)
  local copies, waits for them, and re-layouts  6.59 us (2%)
  other arithmetic  5.16 us (2%)
    reduce_scatter x1, waiting for transfers between devices, body(): lax.psum_scatter(jnp.einsum('aime,mjeb->aijb', screened_right, cycle_weig...  104 us
    psum x1, blocking collectives, body(): lax.psum((numerator_part, correlation), ('blk', 'grp'))  68.5 us
    reduce_scatter x1, waiting for transfers between devices, body(): lax.psum_scatter(product, 'grp', scatter_dimension=0, tiled=True)  62 us
    all_gather x1, waiting for transfers between devices, body(): piece_rows = lax.all_gather(left_vector, 'blk', axis=0, tiled=True)  42 us
    dot_general x1, matrix products, body(): jnp.einsum('kjb,mjeb->kme', flat_rows, cycle_weights, preferred_element_t...  12.9 us
    dot_general x1, matrix products, body(): jnp.einsum('aime,mjeb->aijb', screened_right, cycle_weights, preferred_el...  12.2 us
    dot_general x1, matrix products, body(): jnp.einsum('aijb,aimb->jm', piece_rows, right_vector, preferred_element_t...  10.9 us
  transfers between devices with their start and end apart: 3, of which 3 were waited for; matrix products, arithmetic and copies ran while one was open for 8% of the time, Pallas kernels for 0%

commit v1 on v0

v1 whole, which is shorter than its diff:
```python
import functools

import jax
import jax.numpy as jnp
from jax import lax
from jax.experimental import pallas as pl
from jax.experimental.pallas import tpu as pltpu
from jax.sharding import PartitionSpec as P

MESH = pl.DeviceIdType.MESH
F32 = jnp.float32
BF16 = jnp.bfloat16
I16 = jnp.int16
LEVELS = 32000.0
N_SEM = 96


def dot_nn(a, b):
    return jnp.dot(a, b, preferred_element_type=F32)


def dot_nt(a, b):
    return lax.dot_general(a, b, (((1,), (1,)), ((), ())), preferred_element_type=F32)


def encode(x):
    cols = jnp.max(jnp.abs(x), axis=0, keepdims=True)
    top = functools.reduce(jnp.maximum, [cols[:, i * 128 : (i + 1) * 128] for i in range(6)])
    top = jnp.maximum(top, 1e-30)
    inverse = jnp.concatenate([LEVELS / top] * 6, axis=1)
    return jnp.round(x * inverse).astype(jnp.int32).astype(I16), top * (1.0 / LEVELS)


def decode(q, scale):
    return q.astype(jnp.int32).astype(F32) * jnp.concatenate([scale] * 6, axis=1)


def fold(x):
    rows = functools.reduce(jnp.add, [x[i * 8 : (i + 1) * 8] for i in range(6)])
    return functools.reduce(jnp.add, [rows[:, i * 128 : (i + 1) * 128] for i in range(6)])


def kernel(
    screen_ref, right_hbm, left_hbm, weights_hbm, sr_out, sl_out, ray_out,
    w, r, rs, lg, part, tot, sl,
    zb_s, zb_r, zbs_s, zbs_r,
    ring_s, ring_r, rsc_s, rsc_r,
    zf_s, zf_r, zfs_s, zfs_r,
    ys, yr, yss, ysr,
    hs, hr, hss, hsr,
    sums, xs, ysum,
    load_sem, send_sem, recv_sem, ysend_sem, yrecv_sem,
):
    blk = lax.axis_index("blk")
    grp = lax.axis_index("grp")
    x, zl, c = blk // 4, (blk // 2) % 2, blk % 2
    y, zh = grp // 2, grp % 2
    zo = 1 - zl
    sibling = (blk + 1 - 2 * c, grp)
    z_dev = (blk + 2 - 4 * zl, grp)
    xp_dev = ((blk + 4) % 16, grp)
    xm_dev = ((blk + 12) % 16, grp)
    x2_dev = ((blk + 8) % 16, grp)
    y_devs = [(blk, (grp + 2 * k) % 8) for k in (1, 2, 3)]
    h_dev = (blk, grp + 1 - 2 * zh)

    loads = []

    def load(src, dst):
        copy = pltpu.make_async_copy(src, dst, load_sem.at[len(loads)])
        copy.start()
        loads.append(copy)
        return copy

    def pos(dx, z, core):
        return ((x + dx) % 4) * 4 + z * 2 + core

    here = pos(0, zl, c)
    left_in = load(left_hbm, lg.at[here])
    right_in = load(right_hbm, r)
    weights_in = [[load(weights_hbm.at[m, j], w.at[m, j]) for m in range(2)] for j in range(4)]

    barrier = pltpu.get_barrier_semaphore()
    partners = [sibling, z_dev, xp_dev, xm_dev, x2_dev, h_dev] + y_devs
    for partner in partners:
        pl.semaphore_signal(barrier, inc=1, device_id=partner, device_id_type=MESH)
    pl.semaphore_wait(barrier, len(partners))

    started = []

    def send(src, dst, device):
        k = len(started)
        copy = pltpu.make_async_remote_copy(
            src_ref=src, dst_ref=dst, send_sem=send_sem.at[k], recv_sem=recv_sem.at[k],
            device_id=device, device_id_type=MESH,
        )
        copy.start()
        started.append(copy)
        return copy

    def hand(p, device, js=None):
        ref = lg.at[p] if js is None else lg.at[p, pl.ds(js, 2)]
        return send(ref, ref, device)

    left_in.wait()
    got_xp = hand(here, xp_dev)
    got_xm = hand(here, xm_dev)
    got_z = hand(here, z_dev)
    sib_got = [hand(here, sibling)]

    def right_part(j):
        for copy in weights_in[j]:
            copy.wait()
        acc = dot_nn(rs[0].reshape(768, 768), w[0, j]) + dot_nn(rs[1].reshape(768, 768), w[1, j])
        part[j] = acc.reshape(8, 2, 48, 768)
        return send(part.at[j, :, 1 - c], tot.at[j], sibling)

    def join(j, copy):
        copy.wait_recv()

        def step(k, carry):
            tot[j, k] = tot[j, k] + part[j, k, c]
            return carry

        lax.fori_loop(0, 8, step, 0)

    right_in.wait()
    for m in range(2):
        keep = screen_ref[0, 2 * blk + m].astype(F32).astype(BF16)

        def screen_rows(k, carry, m=m, keep=keep):
            rs[m, k] = r[m, k] * keep
            return carry

        lax.fori_loop(0, 16, screen_rows, 0)
    joined = [right_part(0), right_part(1)]

    zb_got = []
    for j in range(2):
        join(j, joined[j])
        for k in range(4):
            q, scale = encode(tot[j, k * 2 + zo])
            zb_s[j, k] = q
            zbs_s[j, k : k + 1] = scale
        zb_got.append(send(zb_s.at[j], zb_r.at[j], z_dev))
        zb_got.append(send(zbs_s.at[j], zbs_r.at[j], z_dev))

    got_xp.wait_recv()
    fwd_p = hand(pos(-1, zl, c), xp_dev, 0)
    got_xm.wait_recv()
    fwd_m = hand(pos(1, zl, c), xm_dev, 2)
    got_z.wait_recv()
    zgot_xp = hand(pos(0, zo, c), xp_dev)
    zgot_xm = hand(pos(0, zo, c), xm_dev)
    sib_got.append(hand(pos(0, zo, c), sibling))
    sib_near = [hand(pos(-1, zl, c), sibling), hand(pos(1, zl, c), sibling)]

    joined += [right_part(2), right_part(3)]

    sums[0:2] = jnp.zeros((2, 8, 128), F32)
    y_sent = []

    def left_part(chunks):
        rows = [pos(dx, z, core) for dx, z in chunks for core in range(2)]
        for m in range(2):
            acc = None
            for j in range(4):
                block = jnp.concatenate([lg[p, j] for p in rows], axis=0)
                term = dot_nt(block, w[m, j])
                acc = term if acc is None else acc + term
            for i, p in enumerate(rows):
                dx, z = chunks[i // 2]
                slab = acc[i * 48 : (i + 1) * 48]
                sl[dx % 4, z, m, i % 2] = slab
                sums[0] += fold(slab * rs[m, p].astype(F32))
        for dx, z in chunks:
            for m in range(2):
                for core in range(2):
                    q, scale = encode(sl[dx % 4, z, m, core])
                    ys[dx % 4, z, m, core] = q
                    yss[dx % 4, z, m * 2 + core : m * 2 + core + 1] = scale
            owner = (x + dx) % 4
            step = (y + 4 - owner) % 4
            slot = (step + 3) % 4

            def go(dx=dx, z=z, owner=owner, slot=slot):
                for copy in y_copies(dx % 4, z, slot, (blk, owner * 2 + zh)):
                    copy.start()

            pl.when(step != 0)(go)
            y_sent.append((dx % 4, z, step, slot, owner))

    def y_copies(d, z, slot, device):
        return [
            pltpu.make_async_remote_copy(
                src_ref=ys.at[d, z], dst_ref=yr.at[slot, z],
                send_sem=ysend_sem.at[d, z, 0], recv_sem=yrecv_sem.at[slot, z, 0],
                device_id=device, device_id_type=MESH,
            ),
            pltpu.make_async_remote_copy(
                src_ref=yss.at[d, z], dst_ref=ysr.at[slot, z],
                send_sem=ysend_sem.at[d, z, 1], recv_sem=yrecv_sem.at[slot, z, 1],
                device_id=device, device_id_type=MESH,
            ),
        ]

    for copy in sib_got:
        copy.wait_recv()
    left_part([(0, zl), (0, zo)])

    fwd_p.wait_recv()
    fwd_m.wait_recv()
    sib_near.append(hand(pos(2, zl, c), sibling))
    for j in (2, 3):
        join(j, joined[j])
    for copy in sib_near:
        copy.wait_recv()
    left_part([(1, zl), (-1, zl), (2, zl)])

    zgot_xp.wait_recv()
    zfwd_p = hand(pos(-1, zo, c), xp_dev, 0)
    zgot_xm.wait_recv()
    zfwd_m = hand(pos(1, zo, c), xm_dev, 2)
    sib_far = [hand(pos(-1, zo, c), sibling), hand(pos(1, zo, c), sibling)]

    def ring_send(n, kind, block, device):
        q, scale = encode(block)
        ring_s[n, kind] = q
        rsc_s[n, kind, 0:1] = scale
        return [
            send(ring_s.at[n, kind], ring_r.at[n, kind], device),
            send(rsc_s.at[n, kind], rsc_r.at[n, kind], device),
        ]

    def ring_take(n, kind, copies):
        for copy in copies:
            copy.wait_recv()
        return decode(ring_r[n, kind], rsc_r[n, kind, 0:1])

    def xz(dx, z):
        return ((x + dx) % 4) * 2 + z

    def ring_first(n, ja, jb, z):
        hop_p = ring_send(n, 0, tot[ja, xz(2, z)], xp_dev)
        hop_m = ring_send(n, 1, tot[jb, xz(2, z)], xm_dev)
        dir_p = ring_send(n, 2, tot[jb, xz(1, z)], xp_dev)
        dir_m = ring_send(n, 3, tot[ja, xz(-1, z)], xm_dev)
        return hop_p, hop_m, dir_p, dir_m

    def ring_second(n, ja, jb, z, first):
        acc_p = ring_send(n, 4, tot[ja, xz(1, z)] + ring_take(n, 0, first[0]), xp_dev)
        acc_m = ring_send(n, 5, tot[jb, xz(-1, z)] + ring_take(n, 1, first[1]), xm_dev)
        return acc_p, acc_m

    def ring_third(n, ja, jb, z, first, second):
        at = xz(0, z)
        tot[ja, at] = tot[ja, at] + ring_take(n, 3, first[3]) + ring_take(n, 4, second[0])
        tot[jb, at] = tot[jb, at] + ring_take(n, 2, first[2]) + ring_take(n, 5, second[1])

    first0 = ring_first(0, 2, 3, zo)
    first1 = ring_first(1, 2, 3, zl)
    for copy in zb_got:
        copy.wait_recv()
    for j in range(2):
        for k in range(4):
            at = k * 2 + zl
            tot[j, at] = tot[j, at] + decode(zb_r[j, k], zbs_r[j, k : k + 1])
    first2 = ring_first(2, 0, 1, zl)

    zfwd_p.wait_recv()
    zfwd_m.wait_recv()
    sib_far.append(hand(pos(2, zo, c), sibling))
    for copy in sib_far:
        copy.wait_recv()
    left_part([(1, zo), (-1, zo), (2, zo)])

    def pairs():
        for m in range(2):
            def step(p, acc, m=m):
                return acc + fold(lg[p, 2 * c + m].astype(F32) * r[m, p].astype(F32))

            sums[1] += lax.fori_loop(0, 16, step, jnp.zeros((8, 128), F32))

    pl.when(blk // 2 == grp)(pairs)

    second0 = ring_second(0, 2, 3, zo, first0)
    sum_copy = send(sums.at[pl.ds(0, 2)], sums.at[pl.ds(2, 2)], sibling)
    second1 = ring_second(1, 2, 3, zl, first1)
    second2 = ring_second(2, 0, 1, zl, first2)

    sum_copy.wait_recv()
    sums[4:6] = sums[0:2] + sums[2:4]
    sum_copy = send(sums.at[pl.ds(4, 2)], sums.at[pl.ds(6, 2)], z_dev)

    ring_third(0, 2, 3, zo, first0, second0)
    for i, j in enumerate((2, 3)):
        q, scale = encode(tot[j, xz(0, zo)])
        zf_s[i] = q
        zfs_s[i : i + 1] = scale
    zf_got = [send(zf_s, zf_r, z_dev), send(zfs_s, zfs_r, z_dev)]

    sum_copy.wait_recv()
    sums[8:10] = sums[4:6] + sums[6:8]
    sum_copy = send(sums.at[pl.ds(8, 2)], sums.at[pl.ds(10, 2)], h_dev)

    own = (y + 4 - x) % 4
    for k in range(3):
        for z in range(2):
            for copy in y_copies(0, z, k, y_devs[0]):
                copy.wait_recv()

    def y_total(z, m, core):
        total = sl[own, z, m, core]
        for k in range(3):
            at = pl.ds(m * 2 + core, 1)
            total = total + decode(yr[k, z, m, core], ysr[k, z, at])
        return total

    for m in range(2):
        for core in range(2):
            q, scale = encode(y_total(1 - zh, m, core))
            hs[m, core] = q
            hss[m * 2 + core : m * 2 + core + 1] = scale
    h_got = [send(hs, hr, h_dev), send(hss, hsr, h_dev)]

    sum_copy.wait_recv()
    xs[x] = sums[8:10] + sums[10:12]
    x_sums = [send(xs.at[x], xs.at[x], device) for device in (xp_dev, xm_dev, x2_dev)]

    ring_third(1, 2, 3, zl, first1, second1)
    ring_third(2, 0, 1, zl, first2, second2)
    sr_out[0] = tot[0, xz(0, zl)]
    sr_out[1] = tot[1, xz(0, zl)]

    for copy in x_sums:
        copy.wait_recv()
    ysum[y] = xs[0] + xs[1] + xs[2] + xs[3]
    y_sums = [send(ysum.at[y], ysum.at[y], device) for device in y_devs]

    for copy in zf_got:
        copy.wait_recv()
    for i, j in enumerate((2, 3)):
        sr_out[j] = tot[j, xz(0, zl)] + decode(zf_r[i], zfs_r[i : i + 1])

    for copy in h_got:
        copy.wait_recv()
    for m in range(2):
        keep = screen_ref[0, 2 * blk + m].astype(F32)
        for core in range(2):
            at = m * 2 + core
            total = y_total(zh, m, core) + decode(hr[m, core], hsr[at : at + 1])
            sl_out[m, core] = total * keep

    for copy in y_sums:
        copy.wait_recv()
    both = ysum[0] + ysum[1] + ysum[2] + ysum[3]
    numerator = jnp.sum(jnp.sum(both[0], axis=0, keepdims=True), axis=1, keepdims=True)
    denominator = jnp.sum(jnp.sum(both[1], axis=0, keepdims=True), axis=1, keepdims=True)
    ray_out[...] = jnp.broadcast_to(numerator / denominator, (8, 128))

    for copy in started:
        copy.wait_send()
    for d, z, step, slot, owner in y_sent:

        def done(d=d, z=z, slot=slot, owner=owner):
            for copy in y_copies(d, z, slot, (blk, owner * 2 + zh)):
                copy.wait_send()

        pl.when(step != 0)(done)


def body(right_vector, left_vector, cycle_weights, screen):
    right = right_vector.reshape(16, 48, 2, 768).transpose(2, 0, 1, 3)
    left = left_vector.reshape(48, 4, 768).transpose(1, 0, 2)
    anywhere = pl.BlockSpec(memory_space=pl.ANY)
    vmem = pl.BlockSpec(memory_space=pltpu.VMEM)
    scratch = [
        pltpu.VMEM((2, 4, 768, 768), BF16),
        pltpu.VMEM((2, 16, 48, 768), BF16),
        pltpu.VMEM((2, 16, 48, 768), BF16),
        pltpu.VMEM((16, 4, 48, 768), BF16),
        pltpu.VMEM((4, 8, 2, 48, 768), F32),
        pltpu.VMEM((4, 8, 48, 768), F32),
        pltpu.VMEM((4, 2, 2, 2, 48, 768), F32),
        pltpu.VMEM((2, 4, 48, 768), I16),
        pltpu.VMEM((2, 4, 48, 768), I16),
        pltpu.VMEM((2, 8, 128), F32),
        pltpu.VMEM((2, 8, 128), F32),
        pltpu.VMEM((3, 6, 48, 768), I16),
        pltpu.VMEM((3, 6, 48, 768), I16),
        pltpu.VMEM((3, 6, 8, 128), F32),
        pltpu.VMEM((3, 6, 8, 128), F32),
        pltpu.VMEM((2, 48, 768), I16),
        pltpu.VMEM((2, 48, 768), I16),
        pltpu.VMEM((8, 128), F32),
        pltpu.VMEM((8, 128), F32),
        pltpu.VMEM((4, 2, 2, 2, 48, 768), I16),
        pltpu.VMEM((3, 2, 2, 2, 48, 768), I16),
        pltpu.VMEM((4, 2, 8, 128), F32),
        pltpu.VMEM((3, 2, 8, 128), F32),
        pltpu.VMEM((2, 2, 48, 768), I16),
        pltpu.VMEM((2, 2, 48, 768), I16),
        pltpu.VMEM((8, 128), F32),
        pltpu.VMEM((8, 128), F32),
        pltpu.VMEM((12, 8, 128), F32),
        pltpu.VMEM((4, 2, 8, 128), F32),
        pltpu.VMEM((4, 2, 8, 128), F32),
        pltpu.SemaphoreType.DMA((10,)),
        pltpu.SemaphoreType.DMA((N_SEM,)),
        pltpu.SemaphoreType.DMA((N_SEM,)),
        pltpu.SemaphoreType.DMA((4, 2, 2)),
        pltpu.SemaphoreType.DMA((3, 2, 2)),
    ]
    sr, sl, ray = pl.pallas_call(
        kernel,
        out_shape=(
            jax.ShapeDtypeStruct((4, 48, 768), F32),
            jax.ShapeDtypeStruct((2, 2, 48, 768), F32),
            jax.ShapeDtypeStruct((8, 128), F32),
        ),
        in_specs=[pl.BlockSpec(memory_space=pltpu.SMEM), anywhere, anywhere, anywhere],
        out_specs=(vmem, vmem, vmem),
        scratch_shapes=scratch,
        compiler_params=pltpu.CompilerParams(
            collective_id=0, has_side_effects=True, vmem_limit_bytes=60 * 2**20
        ),
        cost_estimate=pl.CostEstimate(
            flops=14_500_000_000, bytes_accessed=13_000_000, transcendentals=0
        ),
    )(screen, right, left, cycle_weights)
    sigma_right = sr.transpose(1, 0, 2)[:, None]
    sigma_left = sl.reshape(2, 96, 768).transpose(1, 0, 2)[:, None]
    return sigma_right, sigma_left, ray[0, :1]


def solution(mesh):
    in_specs = (
        P(None, None, "blk", None),
        P("blk", None, "grp", None),
        P("blk", "grp", None, None),
        P(),
    )
    out_specs = (P("blk", None, "grp", None), P("grp", None, "blk", None), P())
    return jax.shard_map(body, mesh=mesh, in_specs=in_specs, out_specs=out_specs, check_vma=False)
```

time: 342 us -> 84.4 us (0.25)
  the two profiles are of different devices: /device:TPU:0 before, /device:TPU:6 now
where the time goes in v1:
time: 84.4 us; the launch traced here: 84.1 us
  Pallas kernels  72.6 us (86%)
  local copies, waits for them, and re-layouts  10.9 us (13%)
    pallas_call x1, Pallas kernels, body(): pl.pallas_call(kernel, out_shape=(jax.ShapeDtypeStruct((4, 48, 768), F32)...  72.6 us
    unnamed x3, local copies, waits for them, and re-layouts  7.33 us
    reshape x1, local copies, waits for them, and re-layouts, body(): sigma_left = sl.reshape(2, 96, 768).transpose(1, 0, 2)[:, None]  2.33 us

profile of v1, /device:TPU:6, one launch (start us, length us, event | category | flops | bytes accessed | tf_op | source)
XLA Modules:
  0.0 84.1 jit_solution(4785066818868380379)
XLA Ops:
  0.6 1.7 %copy.14 = bf16[48,1,4,768]{3,0,2,1:T(8,128)(2,1)} copy(bf16[48,1,4,768]{3,2,1,0:T(4,128)(2,1)} %param.5) | data formatting | bytes 589824 | tf_op args[1]
  2.3 3.4 %copy.7 = bf16[768,1,2,768]{3,0,2,1:T(8,128)(2,1)} copy(bf16[768,1,2,768]{3,2,1,0:T(2,128)(2,1)} %param.4) | data formatting | bytes 4718592 | tf_op args[0]
  5.7 72.6 %shard_map.67 = (f32[4,48,768]{2,1,0:T(8,128)}, f32[2,2,48,768]{3,2,1,0:T(8,128)}, f32[8,128]{1,0:T(8,128)}) custom-call(s32[1,32]{1,0:T(1,128)} %screen_ref.1, bf16[2,16,48,768]{3,2,1,0:T(8,128)(2,1)} %bitcast.18, bf16[4,48,768]{2,1,0:T(8,128)(2,1)} %bitcast.22, bf16[2,4,768,768]{3,2,1,0:T(8,128)(2,1)} %weights_hbm.1), custom_call_target="tpu_custom_call" | custom-call | flops 14499999744 | bytes 13000000 | tf_op jit(solution)/shard_map/pallas_call | solution.py:414
  78.3 1.2 %slice.3 = f32[1,1]{1,0:T(1,128)} slice(f32[8,128]{1,0:T(8,128)} %get-tuple-element.8), slice={[0:1], [0:1]} | slice | bytes 8 | tf_op jit(solution)/shard_map/slice | solution.py:433
  79.5 2.3 %copy.10 = f32[48,1,4,768]{3,2,1,0:T(4,128)} copy(f32[48,1,4,768]{3,0,2,1:T(8,128)} %bitcast.21) | data formatting | bytes 1179648
  81.8 2.3 %copy.13 = f32[2,96,768]{2,0,1:T(2,128)} copy(f32[2,96,768]{2,1,0:T(8,128)} %bitcast.19) | data formatting | bytes 1179648 | tf_op jit(solution)/shard_map/reshape | solution.py:432

commit v2 on v0

v2 whole, which is shorter than its diff:
```python
import functools

import jax
import jax.numpy as jnp
from jax import lax
from jax.experimental import pallas as pl
from jax.experimental.pallas import tpu as pltpu
from jax.sharding import PartitionSpec as P

MESH = pl.DeviceIdType.MESH
F32 = jnp.float32
BF16 = jnp.bfloat16
I16 = jnp.int16
LEVELS = 32000.0
N_SEM = 120


def dot_nn(a, b):
    return jnp.dot(a, b, preferred_element_type=F32)


def dot_nt(a, b):
    return lax.dot_general(a, b, (((1,), (1,)), ((), ())), preferred_element_type=F32)


def wide(scale):
    return jnp.concatenate([scale] * 6, axis=1)


def band(i):
    return pl.ds(pl.multiple_of(i * 16, 16), 16)


def encode(src, q_ref, scale_ref):
    def top_step(i, top):
        return jnp.maximum(top, jnp.abs(src[band(i)]))

    top = lax.fori_loop(0, 3, top_step, jnp.full((16, 768), 1e-30, F32))
    top = jnp.max(top, axis=0, keepdims=True)
    top = functools.reduce(jnp.maximum, [top[:, i * 128 : (i + 1) * 128] for i in range(6)])
    inverse = wide(LEVELS / top)
    scale_ref[...] = jnp.broadcast_to(top * (1.0 / LEVELS), (8, 128))

    def step(i, carry):
        q_ref[band(i)] = jnp.round(src[band(i)] * inverse).astype(jnp.int32).astype(I16)
        return carry

    lax.fori_loop(0, 3, step, 0)


def decode_add(dst, src, terms, factor=1.0):
    scales = [wide(scale[0:1]) for _, scale in terms]

    def step(i, carry):
        total = src[band(i)]
        for (q, _), scale in zip(terms, scales):
            total = total + q[band(i)].astype(jnp.int32).astype(F32) * scale
        dst[band(i)] = total * factor
        return carry

    lax.fori_loop(0, 3, step, 0)


def fold(x):
    rows = functools.reduce(jnp.add, [x[i * 8 : (i + 1) * 8] for i in range(6)])
    return functools.reduce(jnp.add, [rows[:, i * 128 : (i + 1) * 128] for i in range(6)])


def kernel(
    screen_ref, right_hbm, left_hbm, weights_hbm, sr_out, sl_out, ray_out,
    w, right_raw, left_raw, r, rs, lg, part, tot, sl,
    ring_s, ring_r, rsc_s, rsc_r,
    zf_s, zf_r, zfs_s, zfs_r,
    ys, yr, yh, yss, ysr, yhs,
    hs, hr, hss, hsr,
    sums, xs, ysum, ray,
    load_sem, send_sem, recv_sem, ysend_sem, yrecv_sem, yhop_sem, part_sem,
):
    blk = lax.axis_index("blk")
    grp = lax.axis_index("grp")
    x, zl, c = blk // 4, (blk // 2) % 2, blk % 2
    y, zh = grp // 2, grp % 2
    zo = 1 - zl
    sibling = (blk + 1 - 2 * c, grp)
    z_dev = (blk + 2 - 4 * zl, grp)
    xp_dev = ((blk + 4) % 16, grp)
    xm_dev = ((blk + 12) % 16, grp)
    x2_dev = ((blk + 8) % 16, grp)
    y_devs = [(blk, (grp + 2 * k) % 8) for k in (1, 2, 3)]
    h_dev = (blk, grp + 1 - 2 * zh)

    loads = []

    def load(src, dst):
        copy = pltpu.make_async_copy(src, dst, load_sem.at[len(loads)])
        copy.start()
        loads.append(copy)
        return copy

    def pos(dx, z, core):
        return ((x + dx) % 4) * 4 + z * 2 + core

    here = pos(0, zl, c)
    left_in = load(left_hbm, left_raw)
    right_in = load(right_hbm, right_raw)

    def weight_copy(j, m):
        return pltpu.make_async_copy(weights_hbm.at[m, j], w.at[m, j], load_sem.at[2 + j * 2 + m])

    for j in range(4):
        for m in range(2):
            weight_copy(j, m).start()

    barrier = pltpu.get_barrier_semaphore()
    partners = [sibling, z_dev, xp_dev, xm_dev, x2_dev, h_dev] + y_devs
    for partner in partners:
        pl.semaphore_signal(barrier, inc=1, device_id=partner, device_id_type=MESH)
    left_in.wait()
    for j in range(4):
        lg[here, j] = left_raw[:, j, :]
    pl.semaphore_wait(barrier, len(partners))

    started = []

    def send(src, dst, device):
        k = len(started)
        copy = pltpu.make_async_remote_copy(
            src_ref=src, dst_ref=dst, send_sem=send_sem.at[k], recv_sem=recv_sem.at[k],
            device_id=device, device_id_type=MESH,
        )
        copy.start()
        started.append(copy)
        return copy

    def hand(p, device, j=0, count=4):
        ref = lg.at[p, pl.ds(j, count)]
        return send(ref, ref, device)

    def await_all(copies):
        for copy in copies:
            copy.wait_recv()

    own_xp = [hand(here, xp_dev, 0, 2), hand(here, xp_dev, 2, 2)]
    own_xm = [hand(here, xm_dev, 2, 2), hand(here, xm_dev, 0, 2)]
    own_z = [hand(here, z_dev, 0, 2), hand(here, z_dev, 2, 2)]
    sib_0 = [hand(here, sibling)]
    sib_1 = []

    def part_copy(j):
        return pltpu.make_async_remote_copy(
            src_ref=part.at[j, :, 1 - c], dst_ref=tot.at[j], send_sem=part_sem.at[j, 0],
            recv_sem=part_sem.at[j, 1], device_id=sibling, device_id_type=MESH,
        )

    def right_parts(first, last):
        def step(j, carry):
            acc = dot_nn(rs[0].reshape(768, 768), w[0, j]) + dot_nn(rs[1].reshape(768, 768), w[1, j])
            part[j] = acc.reshape(8, 2, 48, 768)
            part_copy(j).start()
            return carry

        lax.fori_loop(first, last, step, 0)

    def join_parts(first):
        for j in range(first, first + 2):
            part_copy(j).wait_recv()

        def step(k, carry):
            j, at = first + k // 8, k % 8
            tot[j, at] = tot[j, at] + part[j, at, c]
            return carry

        lax.fori_loop(0, 16, step, 0)

    sums[0:2] = jnp.zeros((2, 8, 128), F32)

    def left_rows(chunks, m):
        rows = [pos(dx, z, core) for dx, z in chunks for core in range(2)]
        acc = None
        for j in range(4):
            block = jnp.concatenate([lg[p, j] for p in rows], axis=0)
            term = dot_nt(block, w[m, j])
            acc = term if acc is None else acc + term
        for i in range(len(rows)):
            dx, z = chunks[i // 2]
            sl[dx % 4, z, m, i % 2] = acc[i * 48 : (i + 1) * 48]

    def left_both(chunks):
        def step(m, carry):
            left_rows(chunks, m)
            return carry

        lax.fori_loop(0, 2, step, 0)

    def correlate(chunks):
        for dx, z in chunks:

            def step(k, acc, dx=dx, z=z):
                m, core = k // 2, k % 2
                return acc + fold(sl[dx % 4, z, m, core] * rs[m, pos(dx, z, core)].astype(F32))

            sums[0] += lax.fori_loop(0, 4, step, jnp.zeros((8, 128), F32))

    def role(dx):
        owner = (x + dx) % 4
        step = (y + 4 - owner) % 4
        return owner, step, step // 2

    def y_copies(dx, z, m, dst, dst_scale, sems, device):
        return [
            pltpu.make_async_remote_copy(
                src_ref=ys.at[dx % 4, z, m], dst_ref=dst, send_sem=ysend_sem.at[dx % 4, z, m, 0],
                recv_sem=sems.at[0], device_id=device, device_id_type=MESH,
            ),
            pltpu.make_async_remote_copy(
                src_ref=yss.at[dx % 4, z, m], dst_ref=dst_scale, send_sem=ysend_sem.at[dx % 4, z, m, 1],
                recv_sem=sems.at[1], device_id=device, device_id_type=MESH,
            ),
        ]

    def to_owner(dx, z, m, side, device):
        return y_copies(dx, z, m, yr.at[side, z, m], ysr.at[side, z, m], yrecv_sem.at[side, z, m], device)

    def to_side(dx, z, m, device):
        return y_copies(dx, z, m, yh.at[z, m], yhs.at[z, m], yhop_sem.at[z, m], device)

    def y_encode(d, z, m):
        def step(core, carry):
            encode(sl.at[d, z, m, core], ys.at[d, z, m, core], yss.at[d, z, m, core])
            return carry

        lax.fori_loop(0, 2, step, 0)

    def y_far(dx, z):
        owner, step, side = role(dx)
        d = dx % 4

        def far():
            for m in range(2):
                y_encode(d, z, m)
                for copy in to_side(dx, z, m, y_devs[2 * m]):
                    copy.start()

        pl.when(step == 2)(far)

    def y_near(dx, z):
        owner, step, side = role(dx)
        d = dx % 4

        def near():
            y_encode(d, z, side)
            for copy in to_owner(dx, z, side, side, (blk, owner * 2 + zh)):
                copy.start()

        pl.when(step % 2 == 1)(near)

    def y_second(dx, z):
        owner, step, side = role(dx)
        d = dx % 4
        other = 1 - side

        def near():
            for copy in to_side(dx, z, other, y_devs[0]):
                copy.wait_recv()

            def add(core, carry):
                at = sl.at[d, z, other, core]
                decode_add(at, at, [(yh.at[z, other, core], yhs.at[z, other, core])])
                return carry

            lax.fori_loop(0, 2, add, 0)
            y_encode(d, z, other)
            for copy in to_owner(dx, z, other, side, (blk, owner * 2 + zh)):
                copy.start()

        pl.when(step % 2 == 1)(near)

    def y_drain(dx, z):
        owner, step, side = role(dx)

        def done():
            for m in range(2):
                for copy in to_side(dx, z, m, y_devs[0]):
                    copy.wait_send()

        pl.when(step != 0)(done)

    def first_of(chunks):
        for dx, z in chunks:
            y_far(dx, z)
        for dx, z in chunks:
            y_near(dx, z)

    def second_of(chunks):
        for dx, z in chunks:
            y_second(dx, z)

    def ring_send(n, kind, block, device):
        encode(block, ring_s.at[n, kind], rsc_s.at[n, kind])
        return [
            send(ring_s.at[n, kind], ring_r.at[n, kind], device),
            send(rsc_s.at[n, kind], rsc_r.at[n, kind], device),
        ]

    def ring_add(n, at, kinds):
        for _, copies in kinds:
            await_all(copies)
        decode_add(at, at, [(ring_r.at[n, kind], rsc_r.at[n, kind]) for kind, _ in kinds])

    def xz(dx, z):
        return ((x + dx) % 4) * 2 + z

    def ring_hop(n, ja, jb, z):
        hop_p = ring_send(n, 0, tot.at[ja, xz(2, z)], xp_dev)
        hop_m = ring_send(n, 1, tot.at[jb, xz(2, z)], xm_dev)
        return hop_p, hop_m

    def ring_direct(n, ja, jb, z):
        dir_p = ring_send(n, 2, tot.at[jb, xz(1, z)], xp_dev)
        dir_m = ring_send(n, 3, tot.at[ja, xz(-1, z)], xm_dev)
        return dir_p, dir_m

    def ring_second(n, ja, jb, z, hop):
        to_p, to_m = tot.at[ja, xz(1, z)], tot.at[jb, xz(-1, z)]
        ring_add(n, to_p, [(0, hop[0])])
        acc_p = ring_send(n, 4, to_p, xp_dev)
        ring_add(n, to_m, [(1, hop[1])])
        acc_m = ring_send(n, 5, to_m, xm_dev)
        return acc_p, acc_m

    def ring_third(n, ja, jb, z, direct, second):
        at = xz(0, z)
        ring_add(n, tot.at[ja, at], [(3, direct[1]), (4, second[0])])
        ring_add(n, tot.at[jb, at], [(2, direct[0]), (5, second[1])])

    def z_send(n, ja, jb):
        for i, j in enumerate((ja, jb)):
            encode(tot.at[j, xz(0, zo)], zf_s.at[n, i], zfs_s.at[n, i])
        return [send(zf_s.at[n], zf_r.at[n], z_dev), send(zfs_s.at[n], zfs_r.at[n], z_dev)]

    def z_take(n, ja, jb, copies):
        await_all(copies)
        for i, j in enumerate((ja, jb)):
            at = tot.at[j, xz(0, zl)]
            decode_add(at, at, [(zf_r.at[n, i], zfs_r.at[n, i])])

    right_in.wait()
    for m in range(2):

        def right_rows(k, carry, m=m):
            r[m, k] = right_raw[pl.ds(pl.multiple_of(k * 48, 48), 48), m, :]
            return carry

        lax.fori_loop(0, 16, right_rows, 0)

    own_z[0].wait_recv()
    z_xp = hand(pos(0, zo, c), xp_dev, 0, 2)
    own_xp[0].wait_recv()
    far_xp = hand(pos(-1, zl, c), xp_dev, 0, 2)
    own_xm[0].wait_recv()
    far_xm = hand(pos(1, zl, c), xm_dev, 2, 2)
    z_xm1 = hand(pos(0, zo, c), xm_dev, 1, 1)
    z_xm0 = hand(pos(0, zo, c), xm_dev, 0, 1)
    x_z1 = hand(pos(1, zl, c), z_dev, 2, 2)
    sib_1 += [hand(pos(0, zo, c), sibling, 0, 2), hand(pos(-1, zl, c), sibling, 0, 2)]
    sib_1 += [hand(pos(1, zl, c), sibling, 2, 2)]

    for m in range(2):
        keep = screen_ref[0, 2 * blk + m].astype(F32).astype(BF16)

        def screen_rows(k, carry, m=m, keep=keep):
            rs[m, k] = r[m, k] * keep
            return carry

        lax.fori_loop(0, 16, screen_rows, 0)
    for j in (0, 1):
        for m in range(2):
            weight_copy(j, m).wait()
    right_parts(0, 2)

    own_xp[1].wait_recv()
    x_z2 = hand(pos(-1, zl, c), z_dev, 2, 2)
    own_xm[1].wait_recv()
    own_z[1].wait_recv()
    sib_1 += [hand(pos(0, zo, c), sibling, 2, 2), hand(pos(-1, zl, c), sibling, 2, 2)]
    sib_1 += [hand(pos(1, zl, c), sibling, 0, 2)]

    for j in (2, 3):
        for m in range(2):
            weight_copy(j, m).wait()
    right_parts(2, 4)
    join_parts(0)

    far_xm.wait_recv()
    x_z3 = hand(pos(2, zl, c), z_dev, 2, 2)
    z_xp.wait_recv()
    zfar_xp = hand(pos(-1, zo, c), xp_dev, 0, 1)
    z_xm1.wait_recv()
    zfar_xm = hand(pos(1, zo, c), xm_dev, 1, 1)
    x_z1.wait_recv()
    sib_2 = [hand(pos(-1, zo, c), sibling, 0, 2), hand(pos(1, zo, c), sibling, 2, 2)]
    hop0 = ring_hop(0, 0, 1, zo)
    dir0 = ring_direct(0, 0, 1, zo)

    group0 = [(0, 1 - zh), (0, zh)]
    await_all(sib_0)
    await_all(sib_1)
    left_both(group0)

    far_xp.wait_recv()
    sib_far = hand(pos(2, zl, c), sibling)
    z_xm0.wait_recv()
    x_z2.wait_recv()
    sib_2 += [hand(pos(1, zo, c), sibling, 0, 2), hand(pos(-1, zo, c), sibling, 2, 2)]

    first_of(group0)
    join_parts(2)
    hop2 = ring_hop(2, 2, 3, zo)
    dir2 = ring_direct(2, 2, 3, zo)
    hop1 = ring_hop(1, 0, 1, zl)
    hop3 = ring_hop(3, 2, 3, zl)

    zfar_xp.wait_recv()
    zfar_xm.wait_recv()
    x_z3.wait_recv()
    sib_2.append(hand(pos(2, zo, c), sibling))

    group1 = [(1, zl), (-1, zl), (2, zl)]
    sib_far.wait_recv()
    left_both(group1)
    first_of(group1)
    acc0 = ring_second(0, 0, 1, zo, hop0)
    acc2 = ring_second(2, 2, 3, zo, hop2)
    dir1 = ring_direct(1, 0, 1, zl)
    dir3 = ring_direct(3, 2, 3, zl)

    group2 = [(2, zo), (1, zo), (-1, zo)]
    await_all(sib_2)
    left_both(group2)
    first_of(group2)
    correlate(group0)
    second_of(group0)
    acc1 = ring_second(1, 0, 1, zl, hop1)
    acc3 = ring_second(3, 2, 3, zl, hop3)
    correlate(group1)
    correlate(group2)

    def pairs():
        for m in range(2):

            def step(p, acc, m=m):
                return acc + fold(lg[p, 2 * c + m].astype(F32) * r[m, p].astype(F32))

            sums[1] += lax.fori_loop(0, 16, step, jnp.zeros((8, 128), F32))

    pl.when(blk // 2 == grp)(pairs)
    sum_copy = send(sums.at[pl.ds(0, 2)], sums.at[pl.ds(2, 2)], sibling)

    second_of(group1)

    sum_copy.wait_recv()
    sums[4:6] = sums[0:2] + sums[2:4]
    sum_copy = send(sums.at[pl.ds(4, 2)], sums.at[pl.ds(6, 2)], z_dev)

    ring_third(0, 0, 1, zo, dir0, acc0)
    z_got0 = z_send(0, 0, 1)
    ring_third(2, 2, 3, zo, dir2, acc2)
    z_got1 = z_send(1, 2, 3)

    second_of(group2)

    sum_copy.wait_recv()
    sums[8:10] = sums[4:6] + sums[6:8]
    sum_copy = send(sums.at[pl.ds(8, 2)], sums.at[pl.ds(10, 2)], h_dev)

    own = (y + 4 - x) % 4

    def y_total(z):
        def step(k, carry):
            m, core = k // 2, k % 2
            at = sl.at[own, z, m, core]
            decode_add(at, at, [(yr.at[i, z, m, core], ysr.at[i, z, m, core]) for i in range(2)])
            return carry

        lax.fori_loop(0, 4, step, 0)

    def y_arrived(z):
        for side in range(2):
            for m in range(2):
                for copy in to_owner(0, z, m, side, y_devs[0]):
                    copy.wait_recv()

    y_arrived(1 - zh)
    y_total(1 - zh)

    def h_encode(k, carry):
        m, core = k // 2, k % 2
        encode(sl.at[own, 1 - zh, m, core], hs.at[m, core], hss.at[m, core])
        return carry

    lax.fori_loop(0, 4, h_encode, 0)
    h_got = [send(hs, hr, h_dev), send(hss, hsr, h_dev)]

    sum_copy.wait_recv()
    xs[x] = sums[8:10] + sums[10:12]
    x_sums = [send(xs.at[x], xs.at[x], device) for device in (xp_dev, xm_dev, x2_dev)]

    ring_third(1, 0, 1, zl, dir1, acc1)
    ring_third(3, 2, 3, zl, dir3, acc3)

    await_all(x_sums)
    ysum[y] = xs[0] + xs[1] + xs[2] + xs[3]
    y_sums = [send(ysum.at[y], ysum.at[y], device) for device in y_devs]

    z_take(0, 0, 1, z_got0)
    z_take(1, 2, 3, z_got1)
    sr_copies = []
    for j in range(4):
        copy = pltpu.make_async_copy(tot.at[j, xz(0, zl)], sr_out.at[j], load_sem.at[j])
        copy.start()
        sr_copies.append(copy)

    y_arrived(zh)
    y_total(zh)

    await_all(y_sums)
    both = ysum[0] + ysum[1] + ysum[2] + ysum[3]
    numerator = jnp.sum(jnp.sum(both[0], axis=0, keepdims=True), axis=1, keepdims=True)
    denominator = jnp.sum(jnp.sum(both[1], axis=0, keepdims=True), axis=1, keepdims=True)
    ray[0] = (numerator / denominator)[0, 0]
    ray_copy = pltpu.make_async_copy(ray, ray_out, load_sem.at[8])
    ray_copy.start()

    await_all(h_got)
    sl_copies = []
    for m in range(2):
        keep = screen_ref[0, 2 * blk + m].astype(F32)
        for core in range(2):
            at = sl.at[own, zh, m, core]
            decode_add(at, at, [(hr.at[m, core], hsr.at[m, core])], keep)
            copy = pltpu.make_async_copy(at, sl_out.at[m, core], load_sem.at[4 + m * 2 + core])
            copy.start()
            sl_copies.append(copy)
    for copy in sr_copies + sl_copies + [ray_copy]:
        copy.wait()

    def drain():
        for copy in started:
            copy.wait_send()
        for j in range(4):
            part_copy(j).wait_send()
        for dx, z in group0 + group1 + group2:
            y_drain(dx, z)

    drain()


def body(right_vector, left_vector, cycle_weights, screen):
    right = right_vector.reshape(768, 2, 768)
    left = left_vector.reshape(48, 4, 768)
    anywhere = pl.BlockSpec(memory_space=pl.ANY)
    scratch = [
        pltpu.VMEM((2, 4, 768, 768), BF16),
        pltpu.VMEM((768, 2, 768), BF16),
        pltpu.VMEM((48, 4, 768), BF16),
        pltpu.VMEM((2, 16, 48, 768), BF16),
        pltpu.VMEM((2, 16, 48, 768), BF16),
        pltpu.VMEM((16, 4, 48, 768), BF16),
        pltpu.VMEM((4, 8, 2, 48, 768), F32),
        pltpu.VMEM((4, 8, 48, 768), F32),
        pltpu.VMEM((4, 2, 2, 2, 48, 768), F32),
        pltpu.VMEM((4, 6, 48, 768), I16),
        pltpu.VMEM((4, 6, 48, 768), I16),
        pltpu.VMEM((4, 6, 8, 128), F32),
        pltpu.VMEM((4, 6, 8, 128), F32),
        pltpu.VMEM((2, 2, 48, 768), I16),
        pltpu.VMEM((2, 2, 48, 768), I16),
        pltpu.VMEM((2, 2, 8, 128), F32),
        pltpu.VMEM((2, 2, 8, 128), F32),
        pltpu.VMEM((4, 2, 2, 2, 48, 768), I16),
        pltpu.VMEM((2, 2, 2, 2, 48, 768), I16),
        pltpu.VMEM((2, 2, 2, 48, 768), I16),
        pltpu.VMEM((4, 2, 2, 2, 8, 128), F32),
        pltpu.VMEM((2, 2, 2, 2, 8, 128), F32),
        pltpu.VMEM((2, 2, 2, 8, 128), F32),
        pltpu.VMEM((2, 2, 48, 768), I16),
        pltpu.VMEM((2, 2, 48, 768), I16),
        pltpu.VMEM((2, 2, 8, 128), F32),
        pltpu.VMEM((2, 2, 8, 128), F32),
        pltpu.VMEM((12, 8, 128), F32),
        pltpu.VMEM((4, 2, 8, 128), F32),
        pltpu.VMEM((4, 2, 8, 128), F32),
        pltpu.SMEM((1,), F32),
        pltpu.SemaphoreType.DMA((10,)),
        pltpu.SemaphoreType.DMA((N_SEM,)),
        pltpu.SemaphoreType.DMA((N_SEM,)),
        pltpu.SemaphoreType.DMA((4, 2, 2, 2)),
        pltpu.SemaphoreType.DMA((2, 2, 2, 2)),
        pltpu.SemaphoreType.DMA((2, 2, 2)),
        pltpu.SemaphoreType.DMA((4, 2)),
    ]
    sr, sl, ray = pl.pallas_call(
        kernel,
        out_shape=(
            jax.ShapeDtypeStruct((4, 48, 768), F32),
            jax.ShapeDtypeStruct((2, 2, 48, 768), F32),
            jax.ShapeDtypeStruct((1,), F32),
        ),
        in_specs=[pl.BlockSpec(memory_space=pltpu.SMEM), anywhere, anywhere, anywhere],
        out_specs=(anywhere, anywhere, anywhere),
        scratch_shapes=scratch,
        compiler_params=pltpu.CompilerParams(
            collective_id=0, has_side_effects=True, vmem_limit_bytes=60 * 2**20
        ),
        cost_estimate=pl.CostEstimate(
            flops=14_500_000_000, bytes_accessed=13_000_000, transcendentals=0
        ),
    )(screen, right, left, cycle_weights)
    sigma_right = sr.transpose(1, 0, 2)[:, None]
    sigma_left = sl.reshape(2, 96, 768).transpose(1, 0, 2)[:, None]
    return sigma_right, sigma_left, ray


def solution(mesh):
    in_specs = (
        P(None, None, "blk", None),
        P("blk", None, "grp", None),
        P("blk", "grp", None, None),
        P(),
    )
    out_specs = (P("blk", None, "grp", None), P("grp", None, "blk", None), P())
    return jax.shard_map(body, mesh=mesh, in_specs=in_specs, out_specs=out_specs, check_vma=False)
```

time: 342 us -> 72.4 us (0.21)
  waiting for transfers between devices: 208 us -> 0 us
  blocking collectives: 68.5 us -> 0 us
  Pallas kernels: 0 us -> 64.2 us
  matrix products: 36 us -> 0 us
  between operations: 16.3 us -> 2.39 us
  other arithmetic: 5.16 us -> 0 us
    reduce_scatter x2 -> x0, waiting for transfers between devices: 166 us -> none  [the longest x1 104 us: body(): lax.psum_scatter(jnp.einsum('aime,mjeb->aijb', screened_right, cycle_weig...]
    psum x1 -> x0, blocking collectives: 68.5 us -> none  [body(): lax.psum((numerator_part, correlation), ('blk', 'grp'))]
    pallas_call x0 -> x1, Pallas kernels: none -> 64.2 us  [body(): pl.pallas_call(kernel, out_shape=(jax.ShapeDtypeStruct((4, 48, 768), F32)...]
    all_gather x1 -> x0, waiting for transfers between devices: 42 us -> none  [body(): piece_rows = lax.all_gather(left_vector, 'blk', axis=0, tiled=True)]
    dot_general x3 -> x0, matrix products: 36 us -> none  [the longest x1 12.9 us: body(): jnp.einsum('kjb,mjeb->kme', flat_rows, cycle_weights, preferred_element_t...]
    unnamed x9 -> x1, local copies, waits for them, and re-layouts: 6.59 us -> 2.26 us
  transfers between devices with their start and end apart: 3 -> 0, of which waited for: 3 -> 0; matrix products, arithmetic and copies ran while one was open for 8% -> 0% of each run, Pallas kernels for 0% -> 0%
where the time goes in v2:
time: 72.4 us; the launch traced here: 71.2 us
  Pallas kernels  64.2 us (89%)
  local copies, waits for them, and re-layouts  4.59 us (6%)
  between operations  2.39 us (3%)
    pallas_call x1, Pallas kernels, body(): pl.pallas_call(kernel, out_shape=(jax.ShapeDtypeStruct((4, 48, 768), F32)...  64.2 us
    reshape x1, local copies, waits for them, and re-layouts, body(): sigma_left = sl.reshape(2, 96, 768).transpose(1, 0, 2)[:, None]  2.33 us
    unnamed x1, local copies, waits for them, and re-layouts  2.26 us

profile of v2, /device:TPU:0, one launch (start us, length us, event | category | flops | bytes accessed | tf_op | source)
XLA Modules:
  0.0 71.2 jit_solution(18138722880163450350)
XLA Ops:
  0.6 64.2 %shard_map.67 = (f32[4,48,768]{2,1,0:T(8,128)}, f32[2,2,48,768]{3,2,1,0:T(8,128)}, f32[1]{0:T(128)}) custom-call(s32[1,32]{1,0:T(1,128)} %screen_ref.1, bf16[768,2,768]{2,1,0:T(2,128)(2,1)} %bitcast.14, bf16[48,4,768]{2,1,0:T(4,128)(2,1)} %bitcast.15, bf16[2,4,768,768]{3,2,1,0:T(8,128)(2,1)} %weights_hbm.1), custom_call_target="tpu_custom_call" | custom-call | flops 14499999744 | bytes 13000000 | tf_op jit(solution)/shard_map/pallas_call | solution.py:602
  64.8 2.3 %copy.8 = f32[48,1,4,768]{3,2,1,0:T(4,128)} copy(f32[48,1,4,768]{3,0,2,1:T(8,128)} %bitcast.13) | data formatting | bytes 1179648
  67.1 2.3 %copy.10 = f32[2,96,768]{2,0,1:T(2,128)} copy(f32[2,96,768]{2,1,0:T(8,128)} %bitcast.12) | data formatting | bytes 1179648 | tf_op jit(solution)/shard_map/reshape | solution.py:620

commit v3 on v2

--- a/solution.py
+++ b/solution.py
@@ -12,7 +12,7 @@
 BF16 = jnp.bfloat16
 I16 = jnp.int16
 LEVELS = 32000.0
-N_SEM = 120
+N_SEM = 94
 
 
 def dot_nn(a, b):
@@ -206,71 +206,69 @@
         step = (y + 4 - owner) % 4
         return owner, step, step // 2
 
-    def y_copies(dx, z, m, dst, dst_scale, sems, device):
+    def y_copies(dx, z, m, core, dst, dst_scale, sems, device):
+        at = (dx % 4, z, m, core)
         return [
             pltpu.make_async_remote_copy(
-                src_ref=ys.at[dx % 4, z, m], dst_ref=dst, send_sem=ysend_sem.at[dx % 4, z, m, 0],
-                recv_sem=sems.at[0], device_id=device, device_id_type=MESH,
-            ),
-            pltpu.make_async_remote_copy(
-                src_ref=yss.at[dx % 4, z, m], dst_ref=dst_scale, send_sem=ysend_sem.at[dx % 4, z, m, 1],
-                recv_sem=sems.at[1], device_id=device, device_id_type=MESH,
-            ),
+                src_ref=src.at[at], dst_ref=to, send_sem=ysend_sem.at[at + (i,)], recv_sem=sems.at[i],
+                device_id=device, device_id_type=MESH,
+            )
+            for i, (src, to) in enumerate(((ys, dst), (yss, dst_scale)))
         ]
 
-    def to_owner(dx, z, m, side, device):
-        return y_copies(dx, z, m, yr.at[side, z, m], ysr.at[side, z, m], yrecv_sem.at[side, z, m], device)
-
-    def to_side(dx, z, m, device):
-        return y_copies(dx, z, m, yh.at[z, m], yhs.at[z, m], yhop_sem.at[z, m], device)
-
-    def y_encode(d, z, m):
-        def step(core, carry):
-            encode(sl.at[d, z, m, core], ys.at[d, z, m, core], yss.at[d, z, m, core])
-            return carry
-
-        lax.fori_loop(0, 2, step, 0)
+    def to_owner(dx, z, m, core, side, device):
+        at = (side, z, m, core)
+        return y_copies(dx, z, m, core, yr.at[at], ysr.at[at], yrecv_sem.at[at], device)
+
+    def to_side(dx, z, m, core, device):
+        at = (z, m, core)
+        return y_copies(dx, z, m, core, yh.at[at], yhs.at[at], yhop_sem.at[at], device)
+
+    def y_encode(d, z, m, core):
+        encode(sl.at[d, z, m, core], ys.at[d, z, m, core], yss.at[d, z, m, core])
 
     def y_far(dx, z):
         owner, step, side = role(dx)
-        d = dx % 4
 
         def far():
             for m in range(2):
-                y_encode(d, z, m)
-                for copy in to_side(dx, z, m, y_devs[2 * m]):
-                    copy.start()
+
+                def piece(core, carry, m=m):
+                    y_encode(dx % 4, z, m, core)
+                    for copy in to_side(dx, z, m, core, y_devs[2 * m]):
+                        copy.start()
+                    return carry
+
+                lax.fori_loop(0, 2, piece, 0)
 
         pl.when(step == 2)(far)
 
     def y_near(dx, z):
         owner, step, side = role(dx)
-        d = dx % 4
 
         def near():
-            y_encode(d, z, side)
-            for copy in to_owner(dx, z, side, side, (blk, owner * 2 + zh)):
-                copy.start()
+            def piece(core, carry):
+                y_encode(dx % 4, z, side, core)
+                for copy in to_owner(dx, z, side, core, side, (blk, owner * 2 + zh)):
+                    copy.start()
+                return carry
+
+            lax.fori_loop(0, 2, piece, 0)
 
         pl.when(step % 2 == 1)(near)
 
-    def y_second(dx, z):
+    def y_second(dx, z, core):
         owner, step, side = role(dx)
         d = dx % 4
         other = 1 - side
 
         def near():
-            for copy in to_side(dx, z, other, y_devs[0]):
+            for copy in to_side(dx, z, other, core, y_devs[0]):
                 copy.wait_recv()
-
-            def add(core, carry):
-                at = sl.at[d, z, other, core]
-                decode_add(at, at, [(yh.at[z, other, core], yhs.at[z, other, core])])
-                return carry
-
-            lax.fori_loop(0, 2, add, 0)
-            y_encode(d, z, other)
-            for copy in to_owner(dx, z, other, side, (blk, owner * 2 + zh)):
+            at = sl.at[d, z, other, core]
+            decode_add(at, at, [(yh.at[z, other, core], yhs.at[z, other, core])])
+            y_encode(d, z, other, core)
+            for copy in to_owner(dx, z, other, core, side, (blk, owner * 2 + zh)):
                 copy.start()
 
         pl.when(step % 2 == 1)(near)
@@ -279,9 +277,12 @@
         owner, step, side = role(dx)
 
         def done():
-            for m in range(2):
-                for copy in to_side(dx, z, m, y_devs[0]):
+            def piece(k, carry):
+                for copy in to_side(dx, z, k // 2, k % 2, y_devs[0]):
                     copy.wait_send()
+                return carry
+
+            lax.fori_loop(0, 4, piece, 0)
 
         pl.when(step != 0)(done)
 
@@ -292,8 +293,9 @@
             y_near(dx, z)
 
     def second_of(chunks):
-        for dx, z in chunks:
-            y_second(dx, z)
+        for core in range(2):
+            for dx, z in chunks:
+                y_second(dx, z, core)
 
     def ring_send(n, kind, block, device):
         encode(block, ring_s.at[n, kind], rsc_s.at[n, kind])
@@ -475,31 +477,31 @@
 
     own = (y + 4 - x) % 4
 
-    def y_total(z):
-        def step(k, carry):
-            m, core = k // 2, k % 2
+    def y_total(z, core):
+        for side in range(2):
+            for m in range(2):
+                for copy in to_owner(0, z, m, core, side, y_devs[0]):
+                    copy.wait_recv()
+
+        def step(m, carry):
             at = sl.at[own, z, m, core]
             decode_add(at, at, [(yr.at[i, z, m, core], ysr.at[i, z, m, core]) for i in range(2)])
             return carry
 
-        lax.fori_loop(0, 4, step, 0)
-
-    def y_arrived(z):
-        for side in range(2):
-            for m in range(2):
-                for copy in to_owner(0, z, m, side, y_devs[0]):
-                    copy.wait_recv()
-
-    y_arrived(1 - zh)
-    y_total(1 - zh)
-
-    def h_encode(k, carry):
-        m, core = k // 2, k % 2
-        encode(sl.at[own, 1 - zh, m, core], hs.at[m, core], hss.at[m, core])
-        return carry
-
-    lax.fori_loop(0, 4, h_encode, 0)
-    h_got = [send(hs, hr, h_dev), send(hss, hsr, h_dev)]
+        lax.fori_loop(0, 2, step, 0)
+
+    h_got = []
+    for core in range(2):
+        y_total(1 - zh, core)
+
+        def h_encode(m, carry, core=core):
+            encode(sl.at[own, 1 - zh, m, core], hs.at[core, m], hss.at[core, m])
+            return carry
+
+        lax.fori_loop(0, 2, h_encode, 0)
+        h_got.append(
+            [send(hs.at[core], hr.at[core], h_dev), send(hss.at[core], hsr.at[core], h_dev)]
+        )
 
     sum_copy.wait_recv()
     xs[x] = sums[8:10] + sums[10:12]
@@ -516,12 +518,12 @@
     z_take(1, 2, 3, z_got1)
     sr_copies = []
     for j in range(4):
-        copy = pltpu.make_async_copy(tot.at[j, xz(0, zl)], sr_out.at[j], load_sem.at[j])
+        copy = pltpu.make_async_copy(tot.at[j, xz(0, zl)], sr_out.at[:, j], load_sem.at[j])
         copy.start()
         sr_copies.append(copy)
 
-    y_arrived(zh)
-    y_total(zh)
+    for core in range(2):
+        y_total(zh, core)
 
     await_all(y_sums)
     both = ysum[0] + ysum[1] + ysum[2] + ysum[3]
@@ -531,14 +533,16 @@
     ray_copy = pltpu.make_async_copy(ray, ray_out, load_sem.at[8])
     ray_copy.start()
 
-    await_all(h_got)
     sl_copies = []
-    for m in range(2):
-        keep = screen_ref[0, 2 * blk + m].astype(F32)
-        for core in range(2):
+    for core in range(2):
+        await_all(h_got[core])
+        for m in range(2):
+            keep = screen_ref[0, 2 * blk + m].astype(F32)
             at = sl.at[own, zh, m, core]
-            decode_add(at, at, [(hr.at[m, core], hsr.at[m, core])], keep)
-            copy = pltpu.make_async_copy(at, sl_out.at[m, core], load_sem.at[4 + m * 2 + core])
+            decode_add(at, at, [(hr.at[core, m], hsr.at[core, m])], keep)
+            copy = pltpu.make_async_copy(
+                at, sl_out.at[pl.ds(core * 48, 48), m], load_sem.at[4 + m * 2 + core]
+            )
             copy.start()
             sl_copies.append(copy)
     for copy in sr_copies + sl_copies + [ray_copy]:
@@ -553,6 +557,24 @@
             y_drain(dx, z)
 
     drain()
+
+
+def hand_out(sr_ref, sl_ref, sr_out, sl_out, sr_block, sl_block, sems):
+    into = [
+        pltpu.make_async_copy(sr_ref, sr_block, sems.at[0]),
+        pltpu.make_async_copy(sl_ref, sl_block, sems.at[1]),
+    ]
+    out = [
+        pltpu.make_async_copy(sr_block, sr_out, sems.at[2]),
+        pltpu.make_async_copy(sl_block, sl_out, sems.at[3]),
+    ]
+    for copy in into:
+        copy.start()
+    for first, second in zip(into, out):
+        first.wait()
+        second.start()
+    for copy in out:
+        copy.wait()
 
 
 def body(right_vector, left_vector, cycle_weights, screen):
@@ -594,16 +616,16 @@
         pltpu.SemaphoreType.DMA((10,)),
         pltpu.SemaphoreType.DMA((N_SEM,)),
         pltpu.SemaphoreType.DMA((N_SEM,)),
-        pltpu.SemaphoreType.DMA((4, 2, 2, 2)),
+        pltpu.SemaphoreType.DMA((4, 2, 2, 2, 2)),
+        pltpu.SemaphoreType.DMA((2, 2, 2, 2, 2)),
         pltpu.SemaphoreType.DMA((2, 2, 2, 2)),
-        pltpu.SemaphoreType.DMA((2, 2, 2)),
         pltpu.SemaphoreType.DMA((4, 2)),
     ]
     sr, sl, ray = pl.pallas_call(
         kernel,
         out_shape=(
-            jax.ShapeDtypeStruct((4, 48, 768), F32),
-            jax.ShapeDtypeStruct((2, 2, 48, 768), F32),
+            jax.ShapeDtypeStruct((48, 4, 768), F32),
+            jax.ShapeDtypeStruct((96, 2, 768), F32),
             jax.ShapeDtypeStruct((1,), F32),
         ),
         in_specs=[pl.BlockSpec(memory_space=pltpu.SMEM), anywhere, anywhere, anywhere],
@@ -616,9 +638,18 @@
             flops=14_500_000_000, bytes_accessed=13_000_000, transcendentals=0
         ),
     )(screen, right, left, cycle_weights)
-    sigma_right = sr.transpose(1, 0, 2)[:, None]
-    sigma_left = sl.reshape(2, 96, 768).transpose(1, 0, 2)[:, None]
-    return sigma_right, sigma_left, ray
+    sigma_right, sigma_left = pl.pallas_call(
+        hand_out,
+        out_shape=(jax.ShapeDtypeStruct(sr.shape, F32), jax.ShapeDtypeStruct(sl.shape, F32)),
+        in_specs=[anywhere, anywhere],
+        out_specs=(anywhere, anywhere),
+        scratch_shapes=[
+            pltpu.VMEM(sr.shape, F32),
+            pltpu.VMEM(sl.shape, F32),
+            pltpu.SemaphoreType.DMA((4,)),
+        ],
+    )(sr, sl)
+    return sigma_right[:, None], sigma_left[:, None], ray
 
 
 def solution(mesh):

time: 72.4 us -> 68.8 us (0.950); the launches traced: 71.2 us -> 68.6 us
  local copies, waits for them, and re-layouts: 4.59 us -> 0 us
  Pallas kernels: 64.2 us -> 66.2 us
    reshape x1 -> x0, local copies, waits for them, and re-layouts: 2.33 us -> none  [body(): sigma_left = sl.reshape(2, 96, 768).transpose(1, 0, 2)[:, None]]
    unnamed x1 -> x0, local copies, waits for them, and re-layouts: 2.26 us -> none
    pallas_call x1 -> x2, Pallas kernels: 64.2 us -> 66.2 us  [the longest x1 64.1 us: body(): pl.pallas_call(kernel, out_shape=(jax.ShapeDtypeStruct((48, 4, 768), F32)...]
where the time goes in v3:
time: 68.8 us; the launch traced here: 68.6 us
  Pallas kernels  66.2 us (96%)
  between operations  2.37 us (3%)
    pallas_call x1, Pallas kernels, body(): pl.pallas_call(kernel, out_shape=(jax.ShapeDtypeStruct((48, 4, 768), F32)...  64.1 us
    pallas_call x1, Pallas kernels, body(): pl.pallas_call(hand_out, out_shape=(jax.ShapeDtypeStruct(sr.shape, F32),...  2.11 us

profile of v3, /device:TPU:0, one launch (start us, length us, event | category | flops | bytes accessed | tf_op | source)
XLA Modules:
  0.0 68.6 jit_solution(8326458424412068351)
XLA Ops:
  0.6 64.1 %shard_map.67 = (f32[48,4,768]{2,1,0:T(4,128)}, f32[96,2,768]{2,1,0:T(2,128)}, f32[1]{0:T(128)}) custom-call(s32[1,32]{1,0:T(1,128)} %screen_ref.1, bf16[768,2,768]{2,1,0:T(2,128)(2,1)} %bitcast.8, bf16[48,4,768]{2,1,0:T(4,128)(2,1)} %bitcast.11, bf16[2,4,768,768]{3,2,1,0:T(8,128)(2,1)} %weights_hbm.1), custom_call_target="tpu_custom_call" | custom-call | flops 14499999744 | bytes 13000000 | tf_op jit(solution)/shard_map/pallas_call | solution.py:624
  64.8 2.1 %shard_map.68 = (f32[48,4,768]{2,1,0:T(4,128)}, f32[96,2,768]{2,1,0:T(2,128)}) custom-call(f32[48,4,768]{2,1,0:T(4,128)} %get-tuple-element.8.sr_ref, f32[96,2,768]{2,1,0:T(2,128)} %get-tuple-element.9.sl_ref), custom_call_target="tpu_custom_call" | custom-call | tf_op jit(solution)/shard_map/pallas_call | solution.py:641

commit v4 on v3

--- a/solution.py
+++ b/solution.py
@@ -404,7 +404,7 @@
     hop0 = ring_hop(0, 0, 1, zo)
     dir0 = ring_direct(0, 0, 1, zo)
 
-    group0 = [(0, 1 - zh), (0, zh)]
+    group0 = [(1, zl), (-1, zl), (0, zl)]
     await_all(sib_0)
     await_all(sib_1)
     left_both(group0)
@@ -427,7 +427,7 @@
     x_z3.wait_recv()
     sib_2.append(hand(pos(2, zo, c), sibling))
 
-    group1 = [(1, zl), (-1, zl), (2, zl)]
+    group1 = [(2, zl), (0, zo)]
     sib_far.wait_recv()
     left_both(group1)
     first_of(group1)
@@ -490,6 +490,10 @@
 
         lax.fori_loop(0, 2, step, 0)
 
+    sum_copy.wait_recv()
+    xs[x] = sums[8:10] + sums[10:12]
+    x_sums = [send(xs.at[x], xs.at[x], device) for device in (xp_dev, xm_dev, x2_dev)]
+
     h_got = []
     for core in range(2):
         y_total(1 - zh, core)
@@ -502,10 +506,6 @@
         h_got.append(
             [send(hs.at[core], hr.at[core], h_dev), send(hss.at[core], hsr.at[core], h_dev)]
         )
-
-    sum_copy.wait_recv()
-    xs[x] = sums[8:10] + sums[10:12]
-    x_sums = [send(xs.at[x], xs.at[x], device) for device in (xp_dev, xm_dev, x2_dev)]
 
     ring_third(1, 0, 1, zl, dir1, acc1)
     ring_third(3, 2, 3, zl, dir3, acc3)

time: 68.8 us -> 66.6 us (0.968)
  Pallas kernels: 66.2 us -> 63.9 us
    pallas_call x1, Pallas kernels: 64.1 us -> 61.8 us  [body(): pl.pallas_call(kernel, out_shape=(jax.ShapeDtypeStruct((48, 4, 768), F32)...]
where the time goes in v4:
time: 66.6 us; the launch traced here: 66.2 us
  Pallas kernels  63.9 us (96%)
  between operations  2.37 us (4%)
    pallas_call x1, Pallas kernels, body(): pl.pallas_call(kernel, out_shape=(jax.ShapeDtypeStruct((48, 4, 768), F32)...  61.8 us
    pallas_call x1, Pallas kernels, body(): pl.pallas_call(hand_out, out_shape=(jax.ShapeDtypeStruct(sr.shape, F32),...  2.11 us

profile of v4, /device:TPU:0, one launch (start us, length us, event | category | flops | bytes accessed | tf_op | source)
XLA Modules:
  0.0 66.2 jit_solution(1458574038438307416)
XLA Ops:
  0.6 61.8 %shard_map.67 = (f32[48,4,768]{2,1,0:T(4,128)}, f32[96,2,768]{2,1,0:T(2,128)}, f32[1]{0:T(128)}) custom-call(s32[1,32]{1,0:T(1,128)} %screen_ref.1, bf16[768,2,768]{2,1,0:T(2,128)(2,1)} %bitcast.8, bf16[48,4,768]{2,1,0:T(4,128)(2,1)} %bitcast.11, bf16[2,4,768,768]{3,2,1,0:T(8,128)(2,1)} %weights_hbm.1), custom_call_target="tpu_custom_call" | custom-call | flops 14499999744 | bytes 13000000 | tf_op jit(solution)/shard_map/pallas_call | solution.py:624
  62.4 2.1 %shard_map.68 = (f32[48,4,768]{2,1,0:T(4,128)}, f32[96,2,768]{2,1,0:T(2,128)}) custom-call(f32[48,4,768]{2,1,0:T(4,128)} %get-tuple-element.8.sr_ref, f32[96,2,768]{2,1,0:T(2,128)} %get-tuple-element.9.sl_ref), custom_call_target="tpu_custom_call" | custom-call | tf_op jit(solution)/shard_map/pallas_call | solution.py:641

commit v5 on v4

--- a/solution.py
+++ b/solution.py
@@ -506,13 +506,13 @@
         h_got.append(
             [send(hs.at[core], hr.at[core], h_dev), send(hss.at[core], hsr.at[core], h_dev)]
         )
+        if core == 0:
+            await_all(x_sums)
+            ysum[y] = xs[0] + xs[1] + xs[2] + xs[3]
+            y_sums = [send(ysum.at[y], ysum.at[y], device) for device in y_devs]
 
     ring_third(1, 0, 1, zl, dir1, acc1)
     ring_third(3, 2, 3, zl, dir3, acc3)
-
-    await_all(x_sums)
-    ysum[y] = xs[0] + xs[1] + xs[2] + xs[3]
-    y_sums = [send(ysum.at[y], ysum.at[y], device) for device in y_devs]
 
     z_take(0, 0, 1, z_got0)
     z_take(1, 2, 3, z_got1)

time: 66.6 us -> 66.6 us (level)
  no operation moved by 1% of the time
where the time goes in v5:
time: 66.6 us; the launch traced here: 66.2 us
  Pallas kernels  63.9 us (96%)
  between operations  2.37 us (4%)
    pallas_call x1, Pallas kernels, body(): pl.pallas_call(kernel, out_shape=(jax.ShapeDtypeStruct((48, 4, 768), F32)...  61.8 us
    pallas_call x1, Pallas kernels, body(): pl.pallas_call(hand_out, out_shape=(jax.ShapeDtypeStruct(sr.shape, F32),...  2.11 us

profile of v5, /device:TPU:0, one launch (start us, length us, event | category | flops | bytes accessed | tf_op | source)
XLA Modules:
  0.0 66.2 jit_solution(13938415930815866193)
XLA Ops:
  0.6 61.8 %shard_map.67 = (f32[48,4,768]{2,1,0:T(4,128)}, f32[96,2,768]{2,1,0:T(2,128)}, f32[1]{0:T(128)}) custom-call(s32[1,32]{1,0:T(1,128)} %screen_ref.1, bf16[768,2,768]{2,1,0:T(2,128)(2,1)} %bitcast.8, bf16[48,4,768]{2,1,0:T(4,128)(2,1)} %bitcast.11, bf16[2,4,768,768]{3,2,1,0:T(8,128)(2,1)} %weights_hbm.1), custom_call_target="tpu_custom_call" | custom-call | flops 14499999744 | bytes 13000000 | tf_op jit(solution)/shard_map/pallas_call | solution.py:624
  62.4 2.1 %shard_map.68 = (f32[48,4,768]{2,1,0:T(4,128)}, f32[96,2,768]{2,1,0:T(2,128)}) custom-call(f32[48,4,768]{2,1,0:T(4,128)} %get-tuple-element.8.sr_ref, f32[96,2,768]{2,1,0:T(2,128)} %get-tuple-element.9.sl_ref), custom_call_target="tpu_custom_call" | custom-call | tf_op jit(solution)/shard_map/pallas_call | solution.py:641
